TPU v7x, 256 devices: a whole 4x4x8 slice. The times are simulated.
256 devices in a mesh: teacher: 4 (over y), dp: 16 (over x, z_lo, core), tensor: 4 (over z_hi).
Axes of the slice: x: 4, y: 4, z: 8 (z_hi: 4, z_lo: 2; z = z_hi * 2 + z_lo), core: 2. Of those that a mesh axis runs over, the one named last changes fastest.
Arguments:
- teacher_inputs: bfloat16 [131072, 6144], P(('teacher', 'dp'), 'tensor'), may hold values from -6 to 6
- teacher_keys: bfloat16 [131072, 1024], P(('teacher', 'dp', 'tensor')), may hold values from -6 to 6
- w_key: bfloat16 [1024, 6144], P(('teacher', 'dp'), 'tensor'), may hold values from -0.109375 to 0.109375
- mask_key: int32 [1024, 1536], P(('teacher', 'dp'), 'tensor'), may hold values from 0 to 5
Outputs:
- grad_key: float32 [1024, 6144], P(('teacher', 'dp'), 'tensor')
Inputs may be any that keep to these rules, and one draw needn't show every extreme that they name: `mask_key`: each entry names which two of the four weights of its group along 6144 are kept: 0 keeps positions (0,1), 1 (0,2), 2 (0,3), 3 (1,2), 4 (1,3), 5 (2,3).
All inputs are finite; a program needn't handle non-finite values.
Results may differ from a plain program's by a relative error of at most 0.0011.
Values may be sent and summed in bfloat16 or wider, within the bound.
A program may use at most 192 MiB of HBM per device.

v0:
```python
import math

import jax
import jax.numpy as jnp
from jax import lax
from jax.sharding import PartitionSpec as P


def kept_pair(pattern):
    upper = (pattern >= 3).astype(jnp.int32)
    last = (pattern >= 5).astype(jnp.int32)
    low_pos = upper + last
    high_pos = pattern + 1 - 2 * upper - last
    return [((low_pos == j) | (high_pos == j)).astype(jnp.float32) for j in range(4)]


def expand_last(pattern):
    return jnp.stack(kept_pair(pattern), axis=-1).reshape(pattern.shape[0], -1)


def round_term(values):
    return lax.optimization_barrier(values.astype(jnp.bfloat16)).astype(jnp.float32)


def body(teacher_inputs, teacher_keys, w_key, mask_key):
    kept_mask = expand_last(mask_key)
    masked = w_key * kept_mask.astype(jnp.bfloat16)
    gathered = lax.all_gather(masked, ("teacher", "dp"), axis=0, tiled=True)
    rows_group = teacher_inputs.shape[0]
    sections = lax.axis_size("teacher")
    replicas = lax.axis_size("dp")
    loss_scale = 1.0 / math.sqrt(rows_group * sections * replicas)
    key_cols = gathered.shape[0]
    width_part = gathered.shape[1]
    row_block = teacher_inputs
    product = lax.dot_general(
        row_block, gathered, (((1,), (1,)), ((), ())), preferred_element_type=jnp.float32
    )
    outputs = lax.psum_scatter(round_term(product), "tensor", scatter_dimension=0, tiled=True)
    signal = ((outputs - teacher_keys.astype(jnp.float32)) * loss_scale).astype(jnp.bfloat16)
    row_block = teacher_inputs
    grad_term = lax.dot_general(
        lax.all_gather(signal, "tensor", axis=0, tiled=True),
        row_block,
        (((0,), (0,)), ((), ())),
        preferred_element_type=jnp.float32,
    )
    blocks = round_term(grad_term).reshape(
        sections, replicas, key_cols // (sections * replicas), width_part
    )
    reduced = lax.psum_scatter(blocks, "dp", scatter_dimension=1, tiled=True)
    reduced = lax.psum_scatter(reduced, "teacher", scatter_dimension=0, tiled=True)
    return kept_mask * reduced.reshape(-1, width_part)


def solution(mesh):
    placed = (
        P(("teacher", "dp"), "tensor"),
        P(("teacher", "dp", "tensor"), None),
        P(("teacher", "dp"), "tensor"),
        P(("teacher", "dp"), "tensor"),
    )
    return jax.shard_map(
        body, mesh=mesh, in_specs=placed, out_specs=P(("teacher", "dp"), "tensor"), check_vma=False
    )
```

profile of v0, /device:TPU:24, one launch (start us, length us, event | category | flops | bytes accessed | tf_op | source)
XLA Modules:
  0.0 516.2 jit_solution(7561355538536487687)
XLA Ops:
  6.5 0.8 fusion.6
  7.3 0.3 copy.17
  7.7 0.3 copy.18
  7.9 1.4 fusion
  9.4 0.0 all-gather.3.cloned.1.call-update
  9.4 0.0 reduce-scatter.4.cloned.1.call-start
  9.4 108.9 %all-gather.3.cloned.1.call-done = bf16[1024,1536]{1,0:T(8,128)(2,1)} async-done(((bf16[16,1536]{1,0:T(8,128)(2,1)}), bf16[1024,1536]{1,0:T(8,128)(2,1)}) %all-gather.3.cloned.1.call-update) | async-done | bytes 3145744 | tf_op jit(solution)/shard_map/all_gather | solution.py:28
  118.4 9.8 %convert_bitcast_fusion = bf16[2048,1024]{0,1:T(8,128)(2,1)S(1)} fusion(bf16[1024,1536]{1,0:T(8,128)(2,1)} %all-gather.3.cloned.1.call-done, bf16[2048,1536]{1,0:T(8,128)(2,1)} %param.4), kind=kOutput, calls=%fused_computation | convolution fusion | flops 6444548096 | bytes 13631488 | tf_op jit(solution)/shard_map/dot_general | solution.py:36
  128.1 4.3 convert_element_type.37
  132.5 0.0 all-gather.5.cloned.1.call-start
  132.5 1.1 copy-done
  133.7 0.5 copy.19
  134.2 153.6 %reduce-scatter.4.cloned.1.call-done = f32[512,1024]{0,1:T(8,128)} async-done(((f32[2048,1024]{0,1:T(8,128)}), f32[512,1024]{0,1:T(8,128)}) %reduce-scatter.4.cloned.1.call-update) | async-done | bytes 2097168 | tf_op jit(solution)/shard_map/reduce_scatter | solution.py:39
  287.8 2.9 multiply_convert_fusion
  290.7 0.0 reduce-scatter.6.cloned.1.call-start
  290.8 74.1 %all-gather.5.cloned.1.call-done = bf16[2048,1024]{0,1:T(8,128)(2,1)} async-done(((bf16[512,1024]{0,1:T(8,128)(2,1)}), bf16[2048,1024]{0,1:T(8,128)(2,1)}) %all-gather.5.cloned.1.call-update) | async-done | bytes 4194320 | tf_op jit(solution)/shard_map/all_gather | solution.py:43
  364.9 10.0 %convolution_convert_fusion = bf16[1024,1536]{1,0:T(8,128)(2,1)S(1)} fusion(bf16[2048,1024]{0,1:T(8,128)(2,1)} %all-gather.5.cloned.1.call-done, bf16[2048,1536]{1,0:T(8,128)(2,1)} %param.4), kind=kOutput, calls=%fused_computation.1 | convolution fusion | flops 6444023808 | bytes 13631488 | tf_op jit(solution)/shard_map/dot_general | solution.py:42
  374.9 3.6 copy.20
  378.5 0.0 reduce-scatter.8.cloned.1.call-start
  378.5 88.9 %reduce-scatter.6.cloned.1.call-done = f32[4,1,16,1536]{3,2,0,1:T(8,128)} async-done(((f32[4,16,16,1536]{3,2,0,1:T(8,128)}), f32[4,1,16,1536]{3,2,0,1:T(8,128)}) %reduce-scatter.6.cloned.1.call-update) | async-done | bytes 393232 | tf_op jit(solution)/shard_map/reduce_scatter | solution.py:51
  467.4 3.0 copy.21
  470.5 37.1 %reduce-scatter.8.cloned.1.call-done = f32[1,1,16,1536]{2,3,1,0:T(8,128)} async-done(((f32[4,1,16,1536]{2,3,1,0:T(8,128)}), f32[1,1,16,1536]{2,3,1,0:T(8,128)}) %reduce-scatter.8.cloned.1.call-update) | async-done | bytes 98320 | tf_op jit(solution)/shard_map/reduce_scatter | solution.py:52
  507.6 1.2 bitcast_select_fusion
  508.8 0.9 copy.22
  (7 shorter events, 0.1 us)
Async XLA Ops:
  6.5 111.8 %all-gather.3.cloned.1.call-start = ((), (), s32[]{:S(2)}) async-start(), calls=%async_computation.3 | async-start | bytes 3194880 | tf_op jit(solution)/shard_map/all_gather | solution.py:28
  9.4 278.4 %reduce-scatter.4.cloned.1.call-start = ((), (), s32[]{:S(2)}) async-start(), calls=%async_computation.4 | async-start | bytes 10485760 | tf_op jit(solution)/shard_map/reduce_scatter | solution.py:39
  132.4 1.2 copy-start
  132.5 232.4 %all-gather.5.cloned.1.call-start = ((), (), s32[]{:S(2)}) async-start(), calls=%async_computation.5 | async-start | bytes 5242880 | tf_op jit(solution)/shard_map/all_gather | solution.py:43
  290.7 176.7 %reduce-scatter.6.cloned.1.call-start = ((), (), s32[]{:S(2)}) async-start(), calls=%async_computation.6 | async-start | bytes 6684672 | tf_op jit(solution)/shard_map/reduce_scatter | solution.py:51
  378.5 129.1 %reduce-scatter.8.cloned.1.call-start = ((), (), s32[]{:S(2)}) async-start(), calls=%async_computation.7 | async-start | bytes 3932160 | tf_op jit(solution)/shard_map/reduce_scatter | solution.py:52
Sparse Core Ops, SparseCore 0:
  9.5 108.8 all-gather.2
  132.6 155.1 reduce-scatter.3
  290.8 73.9 all-gather.4
  378.6 88.7 reduce-scatter.5
  470.6 36.9 reduce-scatter.7
where the time goes:
time: 520 us; the launch traced here: 516 us
  waiting for transfers between devices  463 us (89%)
  matrix products  19.8 us (4%)
  between operations  13.2 us (3%)
  other arithmetic  10.6 us (2%)
  local copies, waits for them, and re-layouts  9.77 us (2%)
    reduce_scatter x1, waiting for transfers between devices, body(): lax.psum_scatter(round_term(product), 'tensor', scatter_dimension=0, tile...  154 us
    all_gather x1, waiting for transfers between devices, body(): gathered = lax.all_gather(masked, ('teacher', 'dp'), axis=0, tiled=True)  109 us
    reduce_scatter x1, waiting for transfers between devices, body(): reduced = lax.psum_scatter(blocks, 'dp', scatter_dimension=1, tiled=True)  88.9 us
    all_gather x1, waiting for transfers between devices, body(): lax.all_gather(signal, 'tensor', axis=0, tiled=True)  74.1 us
    reduce_scatter x1, waiting for transfers between devices, body(): lax.psum_scatter(reduced, 'teacher', scatter_dimension=0, tiled=True)  37.1 us
  transfers between devices with their start and end apart: 5, of which 5 were waited for; matrix products, arithmetic and copies ran while one was open for 0% of the time, Pallas kernels for 0%

commit v1 on v0

v1 whole, which is shorter than its diff:
```python
import functools
import math

import jax
import jax.numpy as jnp
from jax import lax
from jax.experimental import pallas as pl
from jax.experimental.pallas import tpu as pltpu
from jax.sharding import PartitionSpec as P

MESH = pl.DeviceIdType.MESH
F32 = jnp.float32
BF16 = jnp.bfloat16
PIECES = 4


def pair(core, t):
    return (1 - core) * (t + 1 - 2 * lax.rem(t, 2)) + core * (3 - t)


def device(y, x, l, c, t):
    return {"teacher": y, "dp": x * 4 + l * 2 + c, "tensor": t}


def kept_of(mask_ref, quarter):
    rows, groups = mask_ref.shape
    pattern = mask_ref[...].astype(F32).astype(BF16)
    spread_row = lax.broadcasted_iota(jnp.int32, (128, 512), 0)
    spread_col = lax.broadcasted_iota(jnp.int32, (128, 512), 1)
    spread = jnp.where(spread_col // 4 == spread_row, 1.0, 0.0).astype(BF16)
    place = (lax.broadcasted_iota(jnp.int32, (rows, 512), 1) % 4).astype(F32)
    parts = []
    for i in range(groups // 128):
        p = jnp.dot(pattern[:, i * 128:(i + 1) * 128], spread, preferred_element_type=F32)
        upper = jnp.where(p > 2.5, 1.0, 0.0)
        last = jnp.where(p > 4.5, 1.0, 0.0)
        low = upper + last
        high = p + 1.0 - 2.0 * upper - last
        parts.append(jnp.where((low == place) | (high == place), 1.0, 0.0))
    return jnp.concatenate(parts, axis=1)


def kernel(scale, x_ref, y_ref, w_ref, mask_ref, o_ref,
           xb, wb, yt, ptf, pb, pr, sb, gb, ar, bs, br, zs, fr, kept, masked,
           x_send, x_recv, x_own, w0_send, w0_recv, wa_send, wa_recv, wb_send, wb_recv,
           p_send, p_recv, a_send, a_recv, b_send, b_recv, f_send, f_recv):
    y = lax.axis_index("teacher")
    d = lax.axis_index("dp")
    t = lax.axis_index("tensor")
    x = lax.div(d, 4)
    l = lax.rem(lax.div(d, 2), 2)
    c = lax.rem(d, 2)
    a = x + c * (y - x)
    b = y + c * (x - y)
    q = pair(c, t)
    u = pair(1 - c, t)
    block_rows, quarter = xb.shape[1], xb.shape[2] // 2
    piece = 2 * quarter // PIECES
    chunk = wb.shape[1] * wb.shape[2]

    def along_a(n):
        other = lax.rem(a + n, 4)
        return other, device(y + c * (other - y), x + (1 - c) * (other - x), l, c, t)

    def along_b(n):
        other = lax.rem(b + n, 4)
        return other, device(y + (1 - c) * (other - y), x + c * (other - x), l, c, t)

    def owner(e):
        return lax.rem(l + lax.div(e, 2), 2), lax.rem(c + lax.rem(e, 2), 2)

    def send(src, dst, ss, rs, to):
        return pltpu.make_async_remote_copy(
            src_ref=src, dst_ref=dst, send_sem=ss, recv_sem=rs, device_id=to, device_id_type=MESH)

    barrier = pltpu.get_barrier_semaphore()
    friends = [along_a(n)[1] for n in (1, 2, 3)] + [along_b(n)[1] for n in (1, 2, 3)]
    friends += [device(y, x, l, c, u)]
    for e in range(4):
        le, ce = owner(jnp.int32(e))
        if e:
            friends.append(device(y, x, le, ce, t))
        friends.append(device(y, x, le, ce, q))
        if e % 2:
            friends.append(device(y, x, le, ce, u))
    for friend in friends:
        pl.semaphore_signal(barrier, 1, device_id=friend, device_id_type=MESH)

    own_copies = []
    for slot, block in ((0, t), (1, u)):
        own_copies.append(pltpu.make_async_copy(
            x_ref.at[pl.ds(block * block_rows, block_rows)], xb.at[slot, :, pl.ds(0, quarter)], x_own.at[slot]))
    kept[...] = kept_of(mask_ref, quarter)
    masked[...] = (w_ref[...].astype(F32) * kept[...]).astype(BF16)
    wb[l * 2 + c, b * 4 + a, :, pl.ds(0, quarter)] = masked[...]

    pl.semaphore_wait(barrier, len(friends))

    w0 = []
    for e in range(4):
        le, ce = owner(jnp.int32(e))
        spot = (y + ce * (x - y)) * 4 + x + ce * (y - x)
        if e:
            w0.append(send(masked, wb.at[l * 2 + c, spot, :, pl.ds(0, quarter)],
                           w0_send.at[0, e], w0_recv.at[0, e], device(y, x, le, ce, t)))
        w0.append(send(masked, wb.at[l * 2 + c, spot, :, pl.ds(quarter, quarter)],
                       w0_send.at[1, e], w0_recv.at[1, e], device(y, x, le, ce, pair(ce, t))))
    for copy in w0:
        copy.start()

    swaps = []
    for slot, block in ((0, q), (1, pair(1 - c, q))):
        swaps.append(send(x_ref.at[pl.ds(block * block_rows, block_rows)], xb.at[slot, :, pl.ds(quarter, quarter)],
                          x_send.at[slot], x_recv.at[slot], device(y, x, l, c, q)))
    for copy in swaps:
        copy.start()
    for copy in own_copies:
        copy.start()

    for copy in w0:
        copy.wait_recv()
    wa = []
    for n in (1, 2, 3):
        wa.append(send(wb.at[:, b * 4 + a], wb.at[:, b * 4 + a], wa_send.at[n - 1], wa_recv.at[n - 1], along_a(n)[1]))
    for copy in wa:
        copy.start()
    for copy in wa:
        copy.wait_recv()
    wg = []
    for n in (1, 2, 3):
        wg.append(send(wb.at[:, pl.ds(b * 4, 4)], wb.at[:, pl.ds(b * 4, 4)],
                       wb_send.at[n - 1], wb_recv.at[n - 1], along_b(n)[1]))
    for copy in wg:
        copy.start()

    def targets(e, carry):
        le, ce = owner(e)
        row = lax.broadcasted_iota(jnp.int32, (chunk, 1), 0)
        row_b, row_a, row_r = row // 64, (row // 16) % 4, row % 16
        key = (row_b + c * (row_a - row_b)) * 256 + (row_a + c * (row_b - row_a)) * 64 + le * 32 + ce * 16 + row_r
        column = lax.broadcasted_iota(jnp.int32, (chunk, y_ref.shape[1]), 1)
        choose = jnp.where(column == key, 1.0, 0.0).astype(BF16)
        yt[e] = lax.dot_general(choose, y_ref[...], (((1,), (1,)), ((), ())),
                                preferred_element_type=F32).astype(BF16)
        return carry

    lax.fori_loop(0, 4, targets, 0)

    for copy in own_copies:
        copy.wait()
    for copy in wg:
        copy.wait_recv()
    for copy in swaps:
        copy.wait_recv()

    def partial_copy(e, slot):
        return send(pb.at[e, slot], pr.at[e, 1 - slot], p_send.at[e, slot], p_recv.at[e, 1 - slot],
                    device(y, x, l, c, u))

    def partials(k, carry):
        e = 3 - k
        le, ce = owner(e)
        rows = wb[le * 2 + ce].reshape(chunk, 2 * quarter)
        for slot in range(2):
            part = lax.dot_general(rows, xb[slot], (((1,), (1,)), ((), ())), preferred_element_type=F32)
            if slot == 0:
                part = part - yt[e].astype(F32)
            ptf[e, slot] = part
            pb[e, slot] = part.astype(BF16)
            partial_copy(e, slot).start()
        return carry

    lax.fori_loop(0, 4, partials, 0)

    def a_copy(e, i, n):
        other, to = along_a(n)
        return send(gb.at[e, :, other, :, pl.ds(i * piece, piece)], ar.at[e, n - 1, :, :, pl.ds(i * piece, piece)],
                    a_send.at[e], a_recv.at[e, i, n - 1], to)

    def b_copy(e, i, n):
        other, to = along_b(n)
        return send(bs.at[e, other, :, pl.ds(i * piece, piece)], br.at[e, n - 1, :, pl.ds(i * piece, piece)],
                    b_send.at[e], b_recv.at[e, i, n - 1], to)

    def f_copy(e, slot):
        le, ce = owner(e)
        return send(zs.at[e, :, pl.ds(slot * quarter, quarter)], fr.at[slot, e],
                    f_send.at[slot, e], f_recv.at[slot, e], device(y, x, le, ce, q if slot else t))

    def gradient(e):
        for slot in range(2):
            partial_copy(e, 1 - slot).wait_recv()
            total = ptf[e, slot] + pr[e, slot].astype(F32)
            sb[:, slot * block_rows:(slot + 1) * block_rows] = (total * scale).astype(BF16)
        for i in range(PIECES):
            rows = xb[:, :, i * piece:(i + 1) * piece].reshape(2 * block_rows, piece)
            term = jnp.dot(sb[...], rows, preferred_element_type=F32)
            gb[e, :, :, :, i * piece:(i + 1) * piece] = term.astype(BF16).reshape(4, 4, 16, piece)
            for n in (1, 2, 3):
                a_copy(e, i, n).start()

    def reduce_a(e):
        for i in range(PIECES):
            cols = slice(i * piece, (i + 1) * piece)
            for n in (1, 2, 3):
                a_copy(e, i, n).wait_recv()
            total = gb[e, :, a, :, cols].astype(F32)
            for n in range(3):
                total = total + ar[e, n, :, :, cols].astype(F32)
            bs[e, :, :, cols] = total.astype(BF16)
            for n in (1, 2, 3):
                b_copy(e, i, n).start()

    def reduce_b(e):
        for i in range(PIECES):
            cols = slice(i * piece, (i + 1) * piece)
            for n in (1, 2, 3):
                b_copy(e, i, n).wait_recv()
            total = bs[e, b, :, cols].astype(F32)
            for n in range(3):
                total = total + br[e, n, :, cols].astype(F32)
            zs[e, :, cols] = total
        f_copy(e, 1).start()

        @pl.when(e > 0)
        def _():
            f_copy(e, 0).start()

    def steps(k, carry):
        @pl.when(k < 4)
        def _():
            gradient(3 - k)

        @pl.when((k >= 1) & (k < 5))
        def _():
            reduce_a(4 - k)

        @pl.when(k >= 2)
        def _():
            reduce_b(5 - k)

        return carry

    lax.fori_loop(0, 6, steps, 0)

    total = zs[0, :, 0:quarter]
    for e in range(4):
        if e:
            f_copy(jnp.int32(e), 0).wait_recv()
            total = total + fr[0, e]
        f_copy(jnp.int32(e), 1).wait_recv()
        total = total + fr[1, e]
    o_ref[...] = kept[...] * total

    for copy in w0 + swaps + wa + wg:
        copy.wait_send()

    def drain(e, carry):
        for slot in range(2):
            partial_copy(e, slot).wait_send()
        pltpu.make_async_copy(ar.at[e], ar.at[e], a_send.at[e]).wait()
        pltpu.make_async_copy(br.at[e], br.at[e], b_send.at[e]).wait()
        f_copy(e, 1).wait_send()

        @pl.when(e > 0)
        def _():
            f_copy(e, 0).wait_send()

        return carry

    lax.fori_loop(0, 4, drain, 0)


def body(teacher_inputs, teacher_keys, w_key, mask_key):
    rows, quarter = teacher_inputs.shape
    block_rows, keys = teacher_keys.shape
    groups = lax.axis_size("teacher") * lax.axis_size("dp")
    scale = 1.0 / math.sqrt(rows * groups)
    width = 2 * quarter
    dma = pltpu.SemaphoreType.DMA
    vmem = pl.BlockSpec(memory_space=pltpu.VMEM)
    return pl.pallas_call(
        functools.partial(kernel, scale),
        out_shape=jax.ShapeDtypeStruct((16, quarter), F32),
        in_specs=[pl.BlockSpec(memory_space=pl.ANY), vmem, vmem, vmem],
        out_specs=vmem,
        scratch_shapes=[
            pltpu.VMEM((2, block_rows, width), BF16),
            pltpu.VMEM((4, 16, 16, width), BF16),
            pltpu.VMEM((4, keys // 4, block_rows), BF16),
            pltpu.VMEM((4, 2, keys // 4, block_rows), F32),
            pltpu.VMEM((4, 2, keys // 4, block_rows), BF16),
            pltpu.VMEM((4, 2, keys // 4, block_rows), BF16),
            pltpu.VMEM((keys // 4, 2 * block_rows), BF16),
            pltpu.VMEM((4, 4, 4, 16, width), BF16),
            pltpu.VMEM((4, 3, 4, 16, width), BF16),
            pltpu.VMEM((4, 4, 16, width), BF16),
            pltpu.VMEM((4, 3, 16, width), BF16),
            pltpu.VMEM((4, 16, width), F32),
            pltpu.VMEM((2, 4, 16, quarter), F32),
            pltpu.VMEM((16, quarter), F32),
            pltpu.VMEM((16, quarter), BF16),
            dma((2,)), dma((2,)), dma((2,)),
            dma((2, 4)), dma((2, 4)),
            dma((3,)), dma((3,)), dma((3,)), dma((3,)),
            dma((4, 2)), dma((4, 2)),
            dma((4,)), dma((4, PIECES, 3)),
            dma((4,)), dma((4, PIECES, 3)),
            dma((2, 4)), dma((2, 4)),
        ],
        compiler_params=pltpu.CompilerParams(
            collective_id=0, has_side_effects=True, vmem_limit_bytes=60 * 2**20),
    )(teacher_inputs, teacher_keys, w_key, mask_key)


def solution(mesh):
    placed = (
        P(("teacher", "dp"), "tensor"),
        P(("teacher", "dp", "tensor"), None),
        P(("teacher", "dp"), "tensor"),
        P(("teacher", "dp"), "tensor"),
    )
    return jax.shard_map(
        body, mesh=mesh, in_specs=placed, out_specs=P(("teacher", "dp"), "tensor"), check_vma=False
    )
```

time: 520 us -> 185 us (0.36)
  waiting for transfers between devices: 463 us -> 0 us
  Pallas kernels: 0 us -> 183 us
  matrix products: 19.8 us -> 0 us
  between operations: 13.2 us -> 0.01 us
  other arithmetic: 10.6 us -> 0 us
  local copies, waits for them, and re-layouts: 9.77 us -> 1.54 us
    reduce_scatter x3 -> x0, waiting for transfers between devices: 280 us -> none  [the longest x1 154 us: body(): lax.psum_scatter(round_term(product), 'tensor', scatter_dimension=0, tile...]
    pallas_call x0 -> x1, Pallas kernels: none -> 183 us  [body(): pl.pallas_call(functools.partial(kernel, scale), out_shape=jax.ShapeDtype...]
    all_gather x2 -> x0, waiting for transfers between devices: 183 us -> none  [the longest x1 109 us: body(): gathered = lax.all_gather(masked, ('teacher', 'dp'), axis=0, tiled=True)]
    dot_general x2 -> x0, matrix products: 19.8 us -> none  [the longest x1 10 us: body(): lax.dot_general(lax.all_gather(signal, 'tensor', axis=0, tiled=True), row...]
    convert_element_type x2 -> x0, other arithmetic: 7.2 us -> none  [the longest x1 4.28 us: round_term(): lax.optimization_barrier(values.astype(jnp.bfloat16)).astype(jnp.float32)]
  transfers between devices with their start and end apart: 5 -> 0, of which waited for: 5 -> 0; matrix products, arithmetic and copies ran while one was open for 0% -> 0% of each run, Pallas kernels for 0% -> 0%
where the time goes in v1:
time: 185 us
  Pallas kernels  183 us (99%)
    pallas_call x1, Pallas kernels, body(): pl.pallas_call(functools.partial(kernel, scale), out_shape=jax.ShapeDtype...  183 us

profile of v1, /device:TPU:24, one launch (start us, length us, event | category | flops | bytes accessed | tf_op | source)
XLA Modules:
  0.0 184.7 jit_solution(371601439519293758)
XLA Ops:
  0.0 183.1 %shard_map.46 = f32[16,1536]{1,0:T(8,128)} custom-call(bf16[2048,1536]{1,0:T(8,128)(2,1)} %x_ref.1, bf16[512,1024]{1,0:T(8,128)(2,1)} %y_ref.1, bf16[16,1536]{1,0:T(8,128)(2,1)} %w_ref.1, s32[16,384]{1,0:T(8,128)} %mask_ref.1), custom_call_target="tpu_custom_call" | custom-call | tf_op jit(solution)/shard_map/pallas_call | solution.py:282
  183.1 1.5 copy.6

commit v2 on v1

v2 whole, which is shorter than its diff:
```python
import functools
import math

import jax
import jax.numpy as jnp
from jax import lax
from jax.experimental import pallas as pl
from jax.experimental.pallas import tpu as pltpu
from jax.sharding import PartitionSpec as P

MESH = pl.DeviceIdType.MESH
F32 = jnp.float32
BF16 = jnp.bfloat16
GROUPS = 128
BLOCK = 4 * GROUPS
PIECES = 3


def pair(core, t):
    return (1 - core) * (t + 1 - 2 * lax.rem(t, 2)) + core * (3 - t)


def device(y, x, l, c, t):
    return {"teacher": y, "dp": x * 4 + l * 2 + c, "tensor": t}


def spread_matrix():
    row = lax.broadcasted_iota(jnp.int32, (GROUPS, BLOCK), 0)
    column = lax.broadcasted_iota(jnp.int32, (GROUPS, BLOCK), 1)
    return jnp.where(column // 4 == row, 1.0, 0.0).astype(BF16)


def squeeze_matrix():
    row = lax.broadcasted_iota(jnp.int32, (BLOCK, GROUPS), 0)
    column = lax.broadcasted_iota(jnp.int32, (BLOCK, GROUPS), 1)
    return jnp.where(row // 4 == column, 1.0, 0.0).astype(BF16)


def kept_places(pattern, spread):
    p = jnp.dot(pattern, spread, preferred_element_type=F32)
    place = (lax.broadcasted_iota(jnp.int32, p.shape, 1) % 4).astype(F32)
    upper = jnp.where(p > 2.5, 1.0, 0.0)
    last = jnp.where(p > 4.5, 1.0, 0.0)
    return upper + last == place, p + 1.0 - 2.0 * upper - last == place


def spread_exactly(values, spread):
    total = None
    for _ in range(3):
        part = values.astype(BF16)
        values = values - part.astype(F32)
        wide = jnp.dot(part, spread, preferred_element_type=F32)
        total = wide if total is None else total + wide
    return total


def kernel(scale, x_ref, y_ref, w_ref, mask_ref, o_ref,
           xb, yb, wc, wb, ml, mh, yt, ptf, pb, pr, sb, gb, ah, ar, bs, bh, br, zs, fr, own,
           x_send, x_recv, x_own, y_own, w0_send, w0_recv, wa_send, wa_recv, wb_send, wb_recv,
           p_send, p_recv, a1_send, a1_recv, a2_send, a2_recv, b1_send, b1_recv, b2_send, b2_recv, f_send, f_recv):
    y = lax.axis_index("teacher")
    d = lax.axis_index("dp")
    t = lax.axis_index("tensor")
    x = lax.div(d, 4)
    l = lax.rem(lax.div(d, 2), 2)
    c = lax.rem(d, 2)
    a = x + c * (y - x)
    b = y + c * (x - y)
    q = pair(c, t)
    u = pair(1 - c, t)
    block_rows, quarter = xb.shape[1], xb.shape[2] // 2
    blocks = quarter // BLOCK
    third = quarter // 4
    packed = 3 * third
    half_width = quarter // 2
    piece = quarter // PIECES
    chunk = wb.shape[1]

    def along_a(n):
        other = lax.rem(a + n, 4)
        return other, device(y + c * (other - y), x + (1 - c) * (other - x), l, c, t)

    def along_b(n):
        other = lax.rem(b + n, 4)
        return other, device(y + (1 - c) * (other - y), x + c * (other - x), l, c, t)

    def owner(e):
        return lax.rem(l + lax.div(e, 2), 2), lax.rem(c + lax.rem(e, 2), 2)

    def send(src, dst, ss, rs, to):
        return pltpu.make_async_remote_copy(
            src_ref=src, dst_ref=dst, send_sem=ss, recv_sem=rs, device_id=to, device_id_type=MESH)

    barrier = pltpu.get_barrier_semaphore()
    friends = [along_a(n)[1] for n in (1, 2, 3)] + [along_b(n)[1] for n in (1, 2, 3)]
    friends += [device(y, x, l, c, u)]
    for e in range(4):
        le, ce = owner(jnp.int32(e))
        if e:
            friends.append(device(y, x, le, ce, t))
        friends.append(device(y, x, le, ce, q))
        if e % 2:
            friends.append(device(y, x, le, ce, u))
    for friend in friends:
        pl.semaphore_signal(barrier, 1, device_id=friend, device_id_type=MESH)

    own_copies = []
    for slot, block in ((0, t), (1, u)):
        own_copies.append(pltpu.make_async_copy(
            x_ref.at[pl.ds(block * block_rows, block_rows)], xb.at[slot, :, pl.ds(0, quarter)], x_own.at[slot]))
    spread, squeeze = spread_matrix(), squeeze_matrix()
    own[:, 2 * third:] = mask_ref[...].astype(F32).astype(BF16)
    for i in range(blocks):
        low, high = kept_places(own[:, 2 * third + i * GROUPS:2 * third + (i + 1) * GROUPS], spread)
        weights = w_ref[:, i * BLOCK:(i + 1) * BLOCK].astype(F32)
        for side, place in enumerate((low, high)):
            own[:, side * third + i * GROUPS:side * third + (i + 1) * GROUPS] = jnp.dot(
                jnp.where(place, weights, 0.0).astype(BF16), squeeze, preferred_element_type=F32).astype(BF16)
    wc[l * 2 + c, b * 4 + a, :, pl.ds(0, packed)] = own[...]

    pl.semaphore_wait(barrier, len(friends))

    w0 = []
    for e in range(4):
        le, ce = owner(jnp.int32(e))
        spot = (y + ce * (x - y)) * 4 + x + ce * (y - x)
        if e:
            w0.append(send(own, wc.at[l * 2 + c, spot, :, pl.ds(0, packed)],
                           w0_send.at[0, e], w0_recv.at[0, e], device(y, x, le, ce, t)))
        w0.append(send(own, wc.at[l * 2 + c, spot, :, pl.ds(packed, packed)],
                       w0_send.at[1, e], w0_recv.at[1, e], device(y, x, le, ce, pair(ce, t))))
    for copy in w0:
        copy.start()

    swaps = []
    for slot, block in ((0, q), (1, pair(1 - c, q))):
        swaps.append(send(x_ref.at[pl.ds(block * block_rows, block_rows)], xb.at[slot, :, pl.ds(quarter, quarter)],
                          x_send.at[slot], x_recv.at[slot], device(y, x, l, c, q)))
    for copy in own_copies:
        copy.start()
    y_copy = pltpu.make_async_copy(y_ref, yb, y_own)
    y_copy.start()

    def to_both(part, ss, rs, along):
        copies = [send(part(0, slice(None)), part(0, slice(None)), ss.at[i], rs.at[i], along(n)[1])
                  for i, n in ((0, 1), (1, 3))]
        for copy in copies:
            copy.start()
        return copies

    def pass_on(part, ss, rs, along):
        copies = [send(part(back, half), part(back, half), ss.at[i], rs.at[i], along(n)[1])
                  for i, n, back, half in ((2, 1, 3, slice(0, 2)), (3, 3, 1, slice(2, 4)))]
        for copy in copies:
            copy.start()
        return copies

    def part_a(n, half):
        return wc.at[half, b * 4 + lax.rem(a + n, 4)]

    def part_b(n, half):
        return wc.at[half, pl.ds(lax.rem(b + n, 4) * 4, 4)]

    for copy in w0:
        copy.wait_recv()
    for copy in swaps:
        copy.start()
    gathers = []
    for part, ss, rs, along in ((part_a, wa_send, wa_recv, along_a), (part_b, wb_send, wb_recv, along_b)):
        first = to_both(part, ss, rs, along)
        for copy in first:
            copy.wait_recv()
        second = pass_on(part, ss, rs, along)
        if part is part_a:
            for copy in second:
                copy.wait_recv()
        gathers += first + second

    def targets(e, carry):
        le, ce = owner(e)
        row = lax.broadcasted_iota(jnp.int32, (chunk, 1), 0)
        row_b, row_a, row_r = row // 64, (row // 16) % 4, row % 16
        key = (row_b + c * (row_a - row_b)) * 256 + (row_a + c * (row_b - row_a)) * 64 + le * 32 + ce * 16 + row_r
        column = lax.broadcasted_iota(jnp.int32, (chunk, yb.shape[1]), 1)
        choose = jnp.where(column == key, 1.0, 0.0).astype(BF16)
        yt[e] = lax.dot_general(choose, yb[...], (((1,), (1,)), ((), ())),
                                preferred_element_type=F32).astype(BF16)
        return carry

    y_copy.wait()
    lax.fori_loop(0, 4, targets, 0)

    for copy in own_copies:
        copy.wait()
    for copy in second:
        copy.wait_recv()

    def unpack(j, carry):
        for i in range(2 * blocks):
            base = i // blocks * packed + i % blocks * GROUPS
            cols = slice(i * BLOCK, (i + 1) * BLOCK)
            parts = [wc[j, :, :, base + side * third:base + side * third + GROUPS].reshape(chunk, GROUPS)
                     for side in range(3)]
            low, high = kept_places(parts[2], spread)
            wide = [jnp.dot(part, spread, preferred_element_type=F32) for part in parts[:2]]
            wb[j, :, cols] = jnp.where(low, wide[0], jnp.where(high, wide[1], 0.0)).astype(BF16)
            ml[j, :, cols] = jnp.where(low, 1.0, 0.0).astype(BF16)
            mh[j, :, cols] = jnp.where(high, 1.0, 0.0).astype(BF16)
        return carry

    lax.fori_loop(0, 4, unpack, 0)
    swaps[0].wait_recv()

    def partial_copy(e, slot):
        return send(pb.at[e, slot], pr.at[e, 1 - slot], p_send.at[e, slot], p_recv.at[e, 1 - slot],
                    device(y, x, l, c, u))

    def partials(k, carry):
        e = 3 - k
        le, ce = owner(e)
        rows = wb[le * 2 + ce]
        for slot in range(2):
            if slot == 1:
                @pl.when(k == 0)
                def _():
                    swaps[1].wait_recv()
            part = lax.dot_general(rows, xb[slot], (((1,), (1,)), ((), ())), preferred_element_type=F32)
            if slot == 0:
                part = part - yt[e].astype(F32)
            ptf[e, slot] = part
            pb[e, slot] = part.astype(BF16)
            partial_copy(e, slot).start()
        return carry

    lax.fori_loop(0, 4, partials, 0)

    def cols_of(i):
        return pl.ds(i * piece, piece)

    def hand(e, i, side, src, dst, ss, rs, along):
        return send(src, dst.at[e, side, :, :, cols_of(i)] if len(dst.shape) == 5 else dst.at[e, side, :, cols_of(i)],
                    ss.at[e], rs.at[e, i, side], along(1 + 2 * side)[1])

    def a_far(e, i, side):
        return hand(e, i, side, gb.at[e, pl.ds(2 * side, 2), lax.rem(a + 2, 4), :, cols_of(i)],
                    ah, a1_send, a1_recv, along_a)

    def a_near(e, i, side):
        return hand(e, i, side, gb.at[e, :, lax.rem(a + 1 + 2 * side, 4), :, cols_of(i)],
                    ar, a2_send, a2_recv, along_a)

    def b_far(e, i, side):
        return hand(e, i, side, bs.at[e, lax.rem(b + 2, 4), pl.ds(8 * side, 8), cols_of(i)],
                    bh, b1_send, b1_recv, along_b)

    def b_near(e, i, side):
        return hand(e, i, side, bs.at[e, lax.rem(b + 1 + 2 * side, 4), :, cols_of(i)],
                    br, b2_send, b2_recv, along_b)

    def f_copy(e, slot):
        le, ce = owner(e)
        return send(zs.at[e, :, pl.ds(slot * half_width, half_width)], fr.at[slot, e],
                    f_send.at[slot, e], f_recv.at[slot, e], device(y, x, le, ce, q if slot else t))

    def gradient(e):
        for slot in range(2):
            partial_copy(e, 1 - slot).wait_recv()
            total = ptf[e, slot] + pr[e, slot].astype(F32)
            sb[:, slot * block_rows:(slot + 1) * block_rows] = (total * scale).astype(BF16)
        le, ce = owner(e)
        j = le * 2 + ce
        for i in range(PIECES):
            wide = slice(i * 2 * piece, (i + 1) * 2 * piece)
            rows = xb[:, :, wide].reshape(2 * block_rows, 2 * piece)
            term = jnp.dot(sb[...], rows, preferred_element_type=F32).astype(BF16)
            kept = []
            for n in range(2 * piece // BLOCK):
                cols = slice(n * BLOCK, (n + 1) * BLOCK)
                spot = slice(i * 2 * piece + n * BLOCK, i * 2 * piece + (n + 1) * BLOCK)
                for place in (ml, mh):
                    kept.append(jnp.dot(term[:, cols] * place[j, :, spot], squeeze, preferred_element_type=F32))
            gb[e, :, :, :, i * piece:(i + 1) * piece] = (
                jnp.concatenate(kept, axis=1).astype(BF16).reshape(4, 4, 16, piece))
            for side in range(2):
                a_far(e, i, side).start()

    def fold_a(e):
        for i in range(PIECES):
            cols = slice(i * piece, (i + 1) * piece)
            for side in range(2):
                a_far(e, i, side).wait_recv()
                spot = lax.rem(a + 1 + 2 * side, 4)
                half = slice(2 * side, 2 * side + 2)
                gb[e, half, spot, :, cols] = (gb[e, half, spot, :, cols].astype(F32)
                                              + ah[e, side, :, :, cols].astype(F32)).astype(BF16)
                a_near(e, i, side).start()

    def reduce_a(e):
        for i in range(PIECES):
            cols = slice(i * piece, (i + 1) * piece)
            total = gb[e, :, a, :, cols].astype(F32)
            for side in range(2):
                a_near(e, i, side).wait_recv()
                total = total + ar[e, side, :, :, cols].astype(F32)
            bs[e, :, :, cols] = total
            for side in range(2):
                b_far(e, i, side).start()

    def fold_b(e):
        for i in range(PIECES):
            cols = slice(i * piece, (i + 1) * piece)
            for side in range(2):
                b_far(e, i, side).wait_recv()
                spot = lax.rem(b + 1 + 2 * side, 4)
                half = slice(8 * side, 8 * side + 8)
                bs[e, spot, half, cols] = bs[e, spot, half, cols] + bh[e, side, :, cols]
                b_near(e, i, side).start()

    def reduce_b(e):
        for i in range(PIECES):
            cols = slice(i * piece, (i + 1) * piece)
            total = bs[e, b, :, cols]
            for side in range(2):
                b_near(e, i, side).wait_recv()
                total = total + br[e, side, :, cols]
            zs[e, :, cols] = total
        f_copy(e, 1).start()

        @pl.when(e > 0)
        def _():
            f_copy(e, 0).start()

    def steps(k, carry):
        @pl.when(k < 4)
        def _():
            gradient(3 - k)

        @pl.when(k >= 1)
        def _():
            fold_b(4 - k)

        @pl.when(k < 4)
        def _():
            fold_a(3 - k)

        @pl.when(k >= 1)
        def _():
            reduce_b(4 - k)

        @pl.when(k < 4)
        def _():
            reduce_a(3 - k)

        return carry

    lax.fori_loop(0, 5, steps, 0)

    total = zs[0, :, 0:half_width]
    for e in range(4):
        if e:
            f_copy(jnp.int32(e), 0).wait_recv()
            total = total + fr[0, e]
        f_copy(jnp.int32(e), 1).wait_recv()
        total = total + fr[1, e]
    for i in range(blocks):
        low, high = kept_places(own[:, 2 * third + i * GROUPS:2 * third + (i + 1) * GROUPS], spread)
        wide = [spread_exactly(total[:, n * GROUPS:(n + 1) * GROUPS], spread) for n in (2 * i, 2 * i + 1)]
        o_ref[:, i * BLOCK:(i + 1) * BLOCK] = jnp.where(low, wide[0], jnp.where(high, wide[1], 0.0))

    for copy in w0 + swaps + gathers:
        copy.wait_send()

    def drain(e, carry):
        for slot in range(2):
            partial_copy(e, slot).wait_send()
        for landed, sent in ((ah, a1_send), (ar, a2_send), (bh, b1_send), (br, b2_send)):
            pltpu.make_async_copy(landed.at[e], landed.at[e], sent.at[e]).wait()
        f_copy(e, 1).wait_send()

        @pl.when(e > 0)
        def _():
            f_copy(e, 0).wait_send()

        return carry

    lax.fori_loop(0, 4, drain, 0)


def body(teacher_inputs, teacher_keys, w_key, mask_key):
    rows, quarter = teacher_inputs.shape
    block_rows, keys = teacher_keys.shape
    groups = lax.axis_size("teacher") * lax.axis_size("dp")
    scale = 1.0 / math.sqrt(rows * groups)
    width = 2 * quarter
    dma = pltpu.SemaphoreType.DMA
    vmem = pl.BlockSpec(memory_space=pltpu.VMEM)
    return pl.pallas_call(
        functools.partial(kernel, scale),
        out_shape=jax.ShapeDtypeStruct((16, quarter), F32),
        in_specs=[pl.BlockSpec(memory_space=pl.ANY), pl.BlockSpec(memory_space=pl.ANY), vmem, vmem],
        out_specs=vmem,
        scratch_shapes=[
            pltpu.VMEM((2, block_rows, width), BF16),
            pltpu.VMEM((block_rows, keys), BF16),
            pltpu.VMEM((4, 16, 16, 3 * width // 4), BF16),
            pltpu.VMEM((4, keys // 4, width), BF16),
            pltpu.VMEM((4, keys // 4, width), BF16),
            pltpu.VMEM((4, keys // 4, width), BF16),
            pltpu.VMEM((4, keys // 4, block_rows), BF16),
            pltpu.VMEM((4, 2, keys // 4, block_rows), F32),
            pltpu.VMEM((4, 2, keys // 4, block_rows), BF16),
            pltpu.VMEM((4, 2, keys // 4, block_rows), BF16),
            pltpu.VMEM((keys // 4, 2 * block_rows), BF16),
            pltpu.VMEM((4, 4, 4, 16, quarter), BF16),
            pltpu.VMEM((4, 2, 2, 16, quarter), BF16),
            pltpu.VMEM((4, 2, 4, 16, quarter), BF16),
            pltpu.VMEM((4, 4, 16, quarter), F32),
            pltpu.VMEM((4, 2, 8, quarter), F32),
            pltpu.VMEM((4, 2, 16, quarter), F32),
            pltpu.VMEM((4, 16, quarter), F32),
            pltpu.VMEM((2, 4, 16, quarter // 2), F32),
            pltpu.VMEM((16, 3 * quarter // 4), BF16),
            dma((2,)), dma((2,)), dma((2,)), dma(()),
            dma((2, 4)), dma((2, 4)),
            dma((4,)), dma((4,)), dma((4,)), dma((4,)),
            dma((4, 2)), dma((4, 2)),
            dma((4,)), dma((4, PIECES, 2)), dma((4,)), dma((4, PIECES, 2)),
            dma((4,)), dma((4, PIECES, 2)), dma((4,)), dma((4, PIECES, 2)),
            dma((2, 4)), dma((2, 4)),
        ],
        compiler_params=pltpu.CompilerParams(
            collective_id=0, has_side_effects=True, vmem_limit_bytes=60 * 2**20),
    )(teacher_inputs, teacher_keys, w_key, mask_key)


def solution(mesh):
    placed = (
        P(("teacher", "dp"), "tensor"),
        P(("teacher", "dp", "tensor"), None),
        P(("teacher", "dp"), "tensor"),
        P(("teacher", "dp"), "tensor"),
    )
    return jax.shard_map(
        body, mesh=mesh, in_specs=placed, out_specs=P(("teacher", "dp"), "tensor"), check_vma=False
    )
```

time: 185 us -> 171 us (0.924); the launches traced: 185 us -> 168 us
  Pallas kernels: 183 us -> 166 us
    pallas_call x1, Pallas kernels: 183 us -> 166 us  [body(): pl.pallas_call(functools.partial(kernel, scale), out_shape=jax.ShapeDtype...]
where the time goes in v2:
time: 171 us; the launch traced here: 168 us
  Pallas kernels  166 us (97%)
    pallas_call x1, Pallas kernels, body(): pl.pallas_call(functools.partial(kernel, scale), out_shape=jax.ShapeDtype...  166 us

profile of v2, /device:TPU:24, one launch (start us, length us, event | category | flops | bytes accessed | tf_op | source)
XLA Modules:
  0.0 167.7 jit_solution(6788710754234535015)
XLA Ops:
  0.0 166.1 %shard_map.46 = f32[16,1536]{1,0:T(8,128)} custom-call(bf16[2048,1536]{1,0:T(8,128)(2,1)} %x_ref.1, bf16[512,1024]{1,0:T(8,128)(2,1)} %y_ref.1, bf16[16,1536]{1,0:T(8,128)(2,1)} %w_ref.1, s32[16,384]{1,0:T(8,128)} %mask_ref.1), custom_call_target="tpu_custom_call" | custom-call | tf_op jit(solution)/shard_map/pallas_call | solution.py:397
  166.1 1.5 copy.6

commit v3 on v2

--- a/solution.py
+++ b/solution.py
@@ -13,7 +13,7 @@
 BF16 = jnp.bfloat16
 GROUPS = 128
 BLOCK = 4 * GROUPS
-PIECES = 3
+PIECES = 2
 
 
 def pair(core, t):
@@ -55,9 +55,9 @@
 
 
 def kernel(scale, x_ref, y_ref, w_ref, mask_ref, o_ref,
-           xb, yb, wc, wb, ml, mh, yt, ptf, pb, pr, sb, gb, ah, ar, bs, bh, br, zs, fr, own,
+           xb, yb, wc, wb, ml, mh, yt, ptf, pb, pr, sb, gb, ar, zs, fr, own,
            x_send, x_recv, x_own, y_own, w0_send, w0_recv, wa_send, wa_recv, wb_send, wb_recv,
-           p_send, p_recv, a1_send, a1_recv, a2_send, a2_recv, b1_send, b1_recv, b2_send, b2_recv, f_send, f_recv):
+           p_send, p_recv, a_send, a_recv, f_send, f_recv):
     y = lax.axis_index("teacher")
     d = lax.axis_index("dp")
     t = lax.axis_index("tensor")
@@ -84,6 +84,11 @@
         other = lax.rem(b + n, 4)
         return other, device(y + (1 - c) * (other - y), x + c * (other - x), l, c, t)
 
+    def across(n):
+        other_a, other_b = lax.rem(a + n % 4, 4), lax.rem(b + n // 4, 4)
+        to = device(other_b + c * (other_a - other_b), other_a + c * (other_b - other_a), l, c, t)
+        return other_b * 4 + other_a, to
+
     def owner(e):
         return lax.rem(l + lax.div(e, 2), 2), lax.rem(c + lax.rem(e, 2), 2)
 
@@ -92,8 +97,7 @@
             src_ref=src, dst_ref=dst, send_sem=ss, recv_sem=rs, device_id=to, device_id_type=MESH)
 
     barrier = pltpu.get_barrier_semaphore()
-    friends = [along_a(n)[1] for n in (1, 2, 3)] + [along_b(n)[1] for n in (1, 2, 3)]
-    friends += [device(y, x, l, c, u)]
+    friends = [across(n)[1] for n in range(1, 16)] + [device(y, x, l, c, u)]
     for e in range(4):
         le, ce = owner(jnp.int32(e))
         if e:
@@ -234,28 +238,19 @@
 
     lax.fori_loop(0, 4, partials, 0)
 
-    def cols_of(i):
-        return pl.ds(i * piece, piece)
-
-    def hand(e, i, side, src, dst, ss, rs, along):
-        return send(src, dst.at[e, side, :, :, cols_of(i)] if len(dst.shape) == 5 else dst.at[e, side, :, cols_of(i)],
-                    ss.at[e], rs.at[e, i, side], along(1 + 2 * side)[1])
-
-    def a_far(e, i, side):
-        return hand(e, i, side, gb.at[e, pl.ds(2 * side, 2), lax.rem(a + 2, 4), :, cols_of(i)],
-                    ah, a1_send, a1_recv, along_a)
-
-    def a_near(e, i, side):
-        return hand(e, i, side, gb.at[e, :, lax.rem(a + 1 + 2 * side, 4), :, cols_of(i)],
-                    ar, a2_send, a2_recv, along_a)
-
-    def b_far(e, i, side):
-        return hand(e, i, side, bs.at[e, lax.rem(b + 2, 4), pl.ds(8 * side, 8), cols_of(i)],
-                    bh, b1_send, b1_recv, along_b)
-
-    def b_near(e, i, side):
-        return hand(e, i, side, bs.at[e, lax.rem(b + 1 + 2 * side, 4), :, cols_of(i)],
-                    br, b2_send, b2_recv, along_b)
+    def spread_out(e, i):
+        cols = pl.ds(i * piece, piece)
+
+        def one(n, carry):
+            spot, to = across(n)
+            send(gb.at[e, spot, :, cols], ar.at[e, n - 1, :, cols], a_send.at[e, i], a_recv.at[e, i], to).start()
+            return carry
+
+        lax.fori_loop(1, 16, one, 0)
+
+    def all_of(e, i, sem):
+        landed = ar.at[e, :, :, pl.ds(i * piece, piece)]
+        return pltpu.make_async_copy(landed, landed, sem.at[e, i])
 
     def f_copy(e, slot):
         le, ce = owner(e)
@@ -269,7 +264,7 @@
             sb[:, slot * block_rows:(slot + 1) * block_rows] = (total * scale).astype(BF16)
         le, ce = owner(e)
         j = le * 2 + ce
-        for i in range(PIECES):
+        for i in reversed(range(PIECES)):
             wide = slice(i * 2 * piece, (i + 1) * 2 * piece)
             rows = xb[:, :, wide].reshape(2 * block_rows, 2 * piece)
             term = jnp.dot(sb[...], rows, preferred_element_type=F32).astype(BF16)
@@ -279,52 +274,20 @@
                 spot = slice(i * 2 * piece + n * BLOCK, i * 2 * piece + (n + 1) * BLOCK)
                 for place in (ml, mh):
                     kept.append(jnp.dot(term[:, cols] * place[j, :, spot], squeeze, preferred_element_type=F32))
-            gb[e, :, :, :, i * piece:(i + 1) * piece] = (
-                jnp.concatenate(kept, axis=1).astype(BF16).reshape(4, 4, 16, piece))
-            for side in range(2):
-                a_far(e, i, side).start()
-
-    def fold_a(e):
-        for i in range(PIECES):
+            gb[e, :, :, i * piece:(i + 1) * piece] = (
+                jnp.concatenate(kept, axis=1).astype(BF16).reshape(16, 16, piece))
+            spread_out(e, i)
+
+    def reduce(e):
+        for i in reversed(range(PIECES)):
             cols = slice(i * piece, (i + 1) * piece)
-            for side in range(2):
-                a_far(e, i, side).wait_recv()
-                spot = lax.rem(a + 1 + 2 * side, 4)
-                half = slice(2 * side, 2 * side + 2)
-                gb[e, half, spot, :, cols] = (gb[e, half, spot, :, cols].astype(F32)
-                                              + ah[e, side, :, :, cols].astype(F32)).astype(BF16)
-                a_near(e, i, side).start()
-
-    def reduce_a(e):
-        for i in range(PIECES):
-            cols = slice(i * piece, (i + 1) * piece)
-            total = gb[e, :, a, :, cols].astype(F32)
-            for side in range(2):
-                a_near(e, i, side).wait_recv()
-                total = total + ar[e, side, :, :, cols].astype(F32)
-            bs[e, :, :, cols] = total
-            for side in range(2):
-                b_far(e, i, side).start()
-
-    def fold_b(e):
-        for i in range(PIECES):
-            cols = slice(i * piece, (i + 1) * piece)
-            for side in range(2):
-                b_far(e, i, side).wait_recv()
-                spot = lax.rem(b + 1 + 2 * side, 4)
-                half = slice(8 * side, 8 * side + 8)
-                bs[e, spot, half, cols] = bs[e, spot, half, cols] + bh[e, side, :, cols]
-                b_near(e, i, side).start()
-
-    def reduce_b(e):
-        for i in range(PIECES):
-            cols = slice(i * piece, (i + 1) * piece)
-            total = bs[e, b, :, cols]
-            for side in range(2):
-                b_near(e, i, side).wait_recv()
-                total = total + br[e, side, :, cols]
+            all_of(e, i, a_recv).wait()
+            total = gb[e, b * 4 + a, :, cols].astype(F32)
+            for n in range(15):
+                total = total + ar[e, n, :, cols].astype(F32)
             zs[e, :, cols] = total
-        f_copy(e, 1).start()
+            if i * piece == half_width:
+                f_copy(e, 1).start()
 
         @pl.when(e > 0)
         def _():
@@ -337,19 +300,7 @@
 
         @pl.when(k >= 1)
         def _():
-            fold_b(4 - k)
-
-        @pl.when(k < 4)
-        def _():
-            fold_a(3 - k)
-
-        @pl.when(k >= 1)
-        def _():
-            reduce_b(4 - k)
-
-        @pl.when(k < 4)
-        def _():
-            reduce_a(3 - k)
+            reduce(4 - k)
 
         return carry
 
@@ -373,8 +324,8 @@
     def drain(e, carry):
         for slot in range(2):
             partial_copy(e, slot).wait_send()
-        for landed, sent in ((ah, a1_send), (ar, a2_send), (bh, b1_send), (br, b2_send)):
-            pltpu.make_async_copy(landed.at[e], landed.at[e], sent.at[e]).wait()
+        for i in range(PIECES):
+            all_of(e, i, a_send).wait()
         f_copy(e, 1).wait_send()
 
         @pl.when(e > 0)
@@ -411,12 +362,8 @@
             pltpu.VMEM((4, 2, keys // 4, block_rows), BF16),
             pltpu.VMEM((4, 2, keys // 4, block_rows), BF16),
             pltpu.VMEM((keys // 4, 2 * block_rows), BF16),
-            pltpu.VMEM((4, 4, 4, 16, quarter), BF16),
-            pltpu.VMEM((4, 2, 2, 16, quarter), BF16),
-            pltpu.VMEM((4, 2, 4, 16, quarter), BF16),
-            pltpu.VMEM((4, 4, 16, quarter), F32),
-            pltpu.VMEM((4, 2, 8, quarter), F32),
-            pltpu.VMEM((4, 2, 16, quarter), F32),
+            pltpu.VMEM((4, 16, 16, quarter), BF16),
+            pltpu.VMEM((4, 15, 16, quarter), BF16),
             pltpu.VMEM((4, 16, quarter), F32),
             pltpu.VMEM((2, 4, 16, quarter // 2), F32),
             pltpu.VMEM((16, 3 * quarter // 4), BF16),
@@ -424,8 +371,7 @@
             dma((2, 4)), dma((2, 4)),
             dma((4,)), dma((4,)), dma((4,)), dma((4,)),
             dma((4, 2)), dma((4, 2)),
-            dma((4,)), dma((4, PIECES, 2)), dma((4,)), dma((4, PIECES, 2)),
-            dma((4,)), dma((4, PIECES, 2)), dma((4,)), dma((4, PIECES, 2)),
+            dma((4, PIECES)), dma((4, PIECES)),
             dma((2, 4)), dma((2, 4)),
         ],
         compiler_params=pltpu.CompilerParams(

time: 171 us -> 157 us (0.918)
  the two profiles are of different devices: /device:TPU:24 before, /device:TPU:61 now
where the time goes in v3:
time: 157 us; the launch traced here: 156 us
  Pallas kernels  155 us (99%)
    pallas_call x1, Pallas kernels, body(): pl.pallas_call(functools.partial(kernel, scale), out_shape=jax.ShapeDtype...  155 us

profile of v3, /device:TPU:61, one launch (start us, length us, event | category | flops | bytes accessed | tf_op | source)
XLA Modules:
  0.0 156.5 jit_solution(14868814889684600827)
XLA Ops:
  0.0 154.9 %shard_map.46 = f32[16,1536]{1,0:T(8,128)} custom-call(bf16[2048,1536]{1,0:T(8,128)(2,1)} %x_ref.1, bf16[512,1024]{1,0:T(8,128)(2,1)} %y_ref.1, bf16[16,1536]{1,0:T(8,128)(2,1)} %w_ref.1, s32[16,384]{1,0:T(8,128)} %mask_ref.1), custom_call_target="tpu_custom_call" | custom-call | tf_op jit(solution)/shard_map/pallas_call | solution.py:348
  154.9 1.5 copy.6

commit v4 on v3

--- a/solution.py
+++ b/solution.py
@@ -55,9 +55,9 @@
 
 
 def kernel(scale, x_ref, y_ref, w_ref, mask_ref, o_ref,
-           xb, yb, wc, wb, ml, mh, yt, ptf, pb, pr, sb, gb, ar, zs, fr, own,
+           xb, yb, wc, wb, ml, mh, yt, ptf, pb, pr, sb, gb, sr, ar, zs, fr, own,
            x_send, x_recv, x_own, y_own, w0_send, w0_recv, wa_send, wa_recv, wb_send, wb_recv,
-           p_send, p_recv, a_send, a_recv, f_send, f_recv):
+           p_send, p_recv, s_send, s_recv, a_send, a_recv, f_send, f_recv):
     y = lax.axis_index("teacher")
     d = lax.axis_index("dp")
     t = lax.axis_index("tensor")
@@ -237,6 +237,10 @@
         return carry
 
     lax.fori_loop(0, 4, partials, 0)
+
+    def across_chip(e):
+        return send(gb.at[e, :, :, pl.ds(0, piece)], sr.at[lax.div(e, 2)], s_send.at[lax.div(e, 2)],
+                    s_recv.at[lax.div(e, 2)], device(y, x, l, 1 - c, t))
 
     def spread_out(e, i):
         cols = pl.ds(i * piece, piece)
@@ -276,20 +280,41 @@
                     kept.append(jnp.dot(term[:, cols] * place[j, :, spot], squeeze, preferred_element_type=F32))
             gb[e, :, :, i * piece:(i + 1) * piece] = (
                 jnp.concatenate(kept, axis=1).astype(BF16).reshape(16, 16, piece))
-            spread_out(e, i)
+            if i:
+                spread_out(e, i)
+
+        odd = lax.rem(e, 2)
+
+        @pl.when(odd == 1)
+        def _():
+            across_chip(e).start()
+
+        @pl.when(odd == 0)
+        def _():
+            across_chip(e).wait_recv()
+            for spot in range(16):
+                other = spot % 4 * 4 + spot // 4
+                gb[e, spot, :, 0:piece] = (gb[e, spot, :, 0:piece].astype(F32)
+                                           + sr[lax.div(e, 2), other].astype(F32)).astype(BF16)
+            spread_out(e, 0)
+
+    def reduce_slot(e, i):
+        cols = slice(i * piece, (i + 1) * piece)
+        all_of(e, i, a_recv).wait()
+        total = gb[e, b * 4 + a, :, cols].astype(F32)
+        for n in range(15):
+            total = total + ar[e, n, :, cols].astype(F32)
+        zs[e, :, cols] = total
 
     def reduce(e):
-        for i in reversed(range(PIECES)):
-            cols = slice(i * piece, (i + 1) * piece)
-            all_of(e, i, a_recv).wait()
-            total = gb[e, b * 4 + a, :, cols].astype(F32)
-            for n in range(15):
-                total = total + ar[e, n, :, cols].astype(F32)
-            zs[e, :, cols] = total
-            if i * piece == half_width:
-                f_copy(e, 1).start()
-
-        @pl.when(e > 0)
+        reduce_slot(e, 1)
+        f_copy(e, 1).start()
+
+        @pl.when(lax.rem(e, 2) == 0)
+        def _():
+            reduce_slot(e, 0)
+
+        @pl.when(e == 2)
         def _():
             f_copy(e, 0).start()
 
@@ -306,35 +331,41 @@
 
     lax.fori_loop(0, 5, steps, 0)
 
-    total = zs[0, :, 0:half_width]
-    for e in range(4):
-        if e:
-            f_copy(jnp.int32(e), 0).wait_recv()
-            total = total + fr[0, e]
+    for copy in w0 + swaps + gathers:
+        copy.wait_send()
+
+    def drain(e, carry):
+        for slot in range(2):
+            partial_copy(e, slot).wait_send()
+        all_of(e, 1, a_send).wait()
+
+        @pl.when(lax.rem(e, 2) == 1)
+        def _():
+            across_chip(e).wait_send()
+
+        @pl.when(lax.rem(e, 2) == 0)
+        def _():
+            all_of(e, 0, a_send).wait()
+
+        @pl.when(e > 0)
+        def _():
+            f_copy(e, 1).wait_send()
+
+        return carry
+
+    lax.fori_loop(0, 4, drain, 0)
+    two = jnp.int32(2)
+    f_copy(two, 0).wait_send()
+    f_copy(two, 0).wait_recv()
+    total = zs[0, :, 0:half_width] + fr[0, 2]
+    for e in (3, 2, 1, 0):
         f_copy(jnp.int32(e), 1).wait_recv()
         total = total + fr[1, e]
     for i in range(blocks):
         low, high = kept_places(own[:, 2 * third + i * GROUPS:2 * third + (i + 1) * GROUPS], spread)
         wide = [spread_exactly(total[:, n * GROUPS:(n + 1) * GROUPS], spread) for n in (2 * i, 2 * i + 1)]
         o_ref[:, i * BLOCK:(i + 1) * BLOCK] = jnp.where(low, wide[0], jnp.where(high, wide[1], 0.0))
-
-    for copy in w0 + swaps + gathers:
-        copy.wait_send()
-
-    def drain(e, carry):
-        for slot in range(2):
-            partial_copy(e, slot).wait_send()
-        for i in range(PIECES):
-            all_of(e, i, a_send).wait()
-        f_copy(e, 1).wait_send()
-
-        @pl.when(e > 0)
-        def _():
-            f_copy(e, 0).wait_send()
-
-        return carry
-
-    lax.fori_loop(0, 4, drain, 0)
+    f_copy(jnp.int32(0), 1).wait_send()
 
 
 def body(teacher_inputs, teacher_keys, w_key, mask_key):
@@ -363,6 +394,7 @@
             pltpu.VMEM((4, 2, keys // 4, block_rows), BF16),
             pltpu.VMEM((keys // 4, 2 * block_rows), BF16),
             pltpu.VMEM((4, 16, 16, quarter), BF16),
+            pltpu.VMEM((2, 16, 16, quarter // 2), BF16),
             pltpu.VMEM((4, 15, 16, quarter), BF16),
             pltpu.VMEM((4, 16, quarter), F32),
             pltpu.VMEM((2, 4, 16, quarter // 2), F32),
@@ -371,6 +403,7 @@
             dma((2, 4)), dma((2, 4)),
             dma((4,)), dma((4,)), dma((4,)), dma((4,)),
             dma((4, 2)), dma((4, 2)),
+            dma((2,)), dma((2,)),
             dma((4, PIECES)), dma((4, PIECES)),
             dma((2, 4)), dma((2, 4)),
         ],

time: 157 us -> 153 us (0.975)
  the two profiles are of different devices: /device:TPU:61 before, /device:TPU:37 now
where the time goes in v4:
time: 153 us
  Pallas kernels  151 us (99%)
  local copies, waits for them, and re-layouts  1.54 us (1%)
    pallas_call x1, Pallas kernels, body(): pl.pallas_call(functools.partial(kernel, scale), out_shape=jax.ShapeDtype...  151 us

profile of v4, /device:TPU:37, one launch (start us, length us, event | category | flops | bytes accessed | tf_op | source)
XLA Modules:
  0.0 152.8 jit_solution(11739786922335729606)
XLA Ops:
  0.0 151.3 %shard_map.46 = f32[16,1536]{1,0:T(8,128)} custom-call(bf16[2048,1536]{1,0:T(8,128)(2,1)} %x_ref.1, bf16[512,1024]{1,0:T(8,128)(2,1)} %y_ref.1, bf16[16,1536]{1,0:T(8,128)(2,1)} %w_ref.1, s32[16,384]{1,0:T(8,128)} %mask_ref.1), custom_call_target="tpu_custom_call" | custom-call | tf_op jit(solution)/shard_map/pallas_call | solution.py:379
  151.3 1.5 %copy.6 = f32[16,1536]{1,0:T(8,128)} copy(f32[16,1536]{1,0:T(8,128)} %shard_map.46) | data formatting | bytes 196608

commit v5 on v4

--- a/solution.py
+++ b/solution.py
@@ -233,7 +233,11 @@
                 part = part - yt[e].astype(F32)
             ptf[e, slot] = part
             pb[e, slot] = part.astype(BF16)
-            partial_copy(e, slot).start()
+
+            @pl.when(k < 2)
+            def _():
+                partial_copy(e, slot).start()
+
         return carry
 
     lax.fori_loop(0, 4, partials, 0)
@@ -266,6 +270,12 @@
             partial_copy(e, 1 - slot).wait_recv()
             total = ptf[e, slot] + pr[e, slot].astype(F32)
             sb[:, slot * block_rows:(slot + 1) * block_rows] = (total * scale).astype(BF16)
+
+        @pl.when(e >= 2)
+        def _():
+            for slot in range(2):
+                partial_copy(e - 2, slot).start()
+
         le, ce = owner(e)
         j = le * 2 + ce
         for i in reversed(range(PIECES)):
@@ -323,13 +333,13 @@
         def _():
             gradient(3 - k)
 
-        @pl.when(k >= 1)
-        def _():
-            reduce(4 - k)
+        @pl.when(k >= 2)
+        def _():
+            reduce(5 - k)
 
         return carry
 
-    lax.fori_loop(0, 5, steps, 0)
+    lax.fori_loop(0, 6, steps, 0)
 
     for copy in w0 + swaps + gathers:
         copy.wait_send()

time: 153 us -> 150 us (0.980)
  the two profiles are of different devices: /device:TPU:37 before, /device:TPU:24 now
where the time goes in v5:
time: 150 us; the launch traced here: 148 us
  Pallas kernels  146 us (97%)
  local copies, waits for them, and re-layouts  1.54 us (1%)
    pallas_call x1, Pallas kernels, body(): pl.pallas_call(functools.partial(kernel, scale), out_shape=jax.ShapeDtype...  146 us

profile of v5, /device:TPU:24, one launch (start us, length us, event | category | flops | bytes accessed | tf_op | source)
XLA Modules:
  0.0 148.0 jit_solution(14146681942337604404)
XLA Ops:
  0.0 146.5 %shard_map.46 = f32[16,1536]{1,0:T(8,128)} custom-call(bf16[2048,1536]{1,0:T(8,128)(2,1)} %x_ref.1, bf16[512,1024]{1,0:T(8,128)(2,1)} %y_ref.1, bf16[16,1536]{1,0:T(8,128)(2,1)} %w_ref.1, s32[16,384]{1,0:T(8,128)} %mask_ref.1), custom_call_target="tpu_custom_call" | custom-call | tf_op jit(solution)/shard_map/pallas_call | solution.py:389
  146.5 1.5 %copy.6 = f32[16,1536]{1,0:T(8,128)} copy(f32[16,1536]{1,0:T(8,128)} %shard_map.46) | data formatting | bytes 196608
